TPU v7x, 32 devices: a whole 2x2x4 slice. The times are simulated.
32 devices in a mesh: clip: 2 (over y), tm: 4 (over z), row: 2 (over x), col: 2 (over core).
Axes of the slice: x: 2, y: 2, z: 4, core: 2. Of those that a mesh axis runs over, the one named last changes fastest.
Arguments:
- right_side: float32 [3, 16, 64, 1024], P(None, ('clip', 'tm'), 'row', 'col'), parts along dimension 1, may hold values from -8 to 8
- screening: float32 [16, 64, 1024], P(('clip', 'tm'), 'row', 'col'), parts along dimension 0, may hold values from 0.05 to 0.5
- time_weight: float32 [16, 64, 1024], P(('clip', 'tm'), 'row', 'col'), parts along dimension 0, may hold values from 0.2 to 5
- row_weight: float32 [16, 64, 1024], P(('clip', 'tm'), 'row', 'col'), parts along dimension 0, may hold values from 0.2 to 5
- column_weight: float32 [16, 64, 1024], P(('clip', 'tm'), 'row', 'col'), parts along dimension 0, may hold values from 0.2 to 5
Outputs:
- solution_field: float32 [3, 16, 64, 1024], P(None, ('clip', 'tm'), 'row', 'col'), parts along dimension 1
- residual: float32 [3, 16, 64, 1024], P(None, ('clip', 'tm'), 'row', 'col'), parts along dimension 1
There are 2 independent parts, one for each index of `clip`. A program takes and returns all parts, laid end to end along the dimension named above; each array names one. Nothing has to cross between parts.
All inputs are finite; a program needn't handle non-finite values.
Results may differ from a plain program's by a relative error of at most 0.0001.
Values sent between devices are 32-bit elements; how exact they have to be, the bound alone decides.
A program may use at most 64 MiB of HBM per device.

v0:
```python
import jax
import jax.numpy as jnp
from jax import lax
from jax.sharding import PartitionSpec as P

ITERS = 2


def padded_2(value, sides, width):
    for axis, dim in sides:
        devices, length = (lax.axis_size(axis), value.shape[dim])
        up = [(i, (i + 1) % devices) for i in range(devices)]
        down = [(j, i) for i, j in up]
        last = lax.slice_in_dim(value, length - width, length, axis=dim)
        leading = lax.slice_in_dim(value, 0, width, axis=dim)
        before = lax.ppermute(last, axis, up)
        after = lax.ppermute(leading, axis, down)
        value = jnp.concatenate([before, value, after], axis=dim)
    return value


def shifted(value, axis, by):
    devices = lax.axis_size(axis)
    return lax.ppermute(value, axis, [(i, (i + by) % devices) for i in range(devices)])


def passed_along(block, axis, distance):
    devices = range(lax.axis_size(axis))
    route = [(i - distance, i) for i in devices if i - distance in devices]
    return lax.ppermute(block, axis, route)


def neighbours(field):
    padded = padded_2(field, (("tm", 1), ("row", 2), ("col", 3)), 1)
    after_time = padded[:, 2:, 1:-1, 1:-1]
    prior_time = padded[:, :-2, 1:-1, 1:-1]
    after_row = padded[:, 1:-1, 2:, 1:-1]
    prior_row = padded[:, 1:-1, :-2, 1:-1]
    after_col = padded[:, 1:-1, 1:-1, 2:]
    prior_col = padded[:, 1:-1, 1:-1, :-2]
    return (after_time, prior_time, after_row, prior_row, after_col, prior_col)


def operate(field, screening, weights):
    wt, before_time, wy, before_row, wx, before_col = weights
    after_time, prior_time, after_row, prior_row, after_col, prior_col = neighbours(field)
    total = screening * field
    total = total + wt * (field - after_time)
    total = total + before_time * (field - prior_time)
    total = total + wy * (field - after_row)
    total = total + before_row * (field - prior_row)
    total = total + wx * (field - after_col)
    total = total + before_col * (field - prior_col)
    return total


def channel_sum(left, right):
    return jnp.sum(left * right, axis=(1, 2, 3))


def expand(scalar):
    return scalar[:, None, None, None]


def squares(residual):
    return lax.psum(channel_sum(residual, residual), ("tm", "row", "col"))


def shards(right_side, screening, time_weight, row_weight, column_weight):
    frames, rows, columns = time_weight.shape
    last_band = lax.axis_index("row") == lax.axis_size("row") - 1
    last_strip = lax.axis_index("col") == lax.axis_size("col") - 1
    row_ids = lax.broadcasted_iota(jnp.int32, (frames, rows, columns), 1)
    col_ids = lax.broadcasted_iota(jnp.int32, (frames, rows, columns), 2)
    wy = jnp.where(jnp.logical_and(last_band, row_ids == rows - 1), 0.0, row_weight)
    wx = jnp.where(jnp.logical_and(last_strip, col_ids == columns - 1), 0.0, column_weight)
    time_rim = shifted(time_weight[-1:], "tm", 1)
    band_rim = passed_along(wy[:, -1:, :], "row", 1)
    strip_rim = passed_along(wx[:, :, -1:], "col", 1)
    before_time = jnp.concatenate([time_rim, time_weight[:-1]], axis=0)
    before_row = jnp.concatenate([band_rim, wy[:, :-1, :]], axis=1)
    before_col = jnp.concatenate([strip_rim, wx[:, :, :-1]], axis=2)
    weights = (time_weight, before_time, wy, before_row, wx, before_col)
    solution_field = jnp.zeros_like(right_side)
    residual = right_side
    direction = right_side
    norm_now = squares(residual)
    for step in range(ITERS):
        image = operate(direction, screening, weights)
        product = lax.psum(channel_sum(direction, image), ("tm", "row", "col"))
        alpha = norm_now / product
        solution_field = solution_field + expand(alpha) * direction
        residual = residual - expand(alpha) * image
        norm_next = squares(residual)
        direction = residual + expand(norm_next / norm_now) * direction
        norm_now = norm_next
    return (solution_field, residual)


def solution(mesh):
    placed = (
        P(None, ("clip", "tm"), "row", "col"),
        P(("clip", "tm"), "row", "col"),
        P(("clip", "tm"), "row", "col"),
        P(("clip", "tm"), "row", "col"),
        P(("clip", "tm"), "row", "col"),
    )
    return jax.shard_map(
        shards,
        mesh=mesh,
        in_specs=placed,
        out_specs=(P(None, ("clip", "tm"), "row", "col"), P(None, ("clip", "tm"), "row", "col")),
        check_vma=False,
    )
```

profile of v0, /device:TPU:0, one launch (start us, length us, event | category | flops | bytes accessed | tf_op | source)
XLA Modules:
  0.0 143.5 jit_solution(11609135693439904314)
XLA Ops:
  0.7 1.0 broadcast_select_fusion.1
  1.7 4.8 %collective-permute-start.4 = (f32[2,1,512]{2,1,0:T(1,128)S(1)}, f32[2,1,512]{2,1,0:T(1,128)S(1)}, u32[]{:S(2)}, u32[]{:S(2)}) collective-permute-start(f32[2,1,512]{2,1,0:T(1,128)S(1)} %slice.133), channel_id=1, source_target_pairs={{0,2},{1,3},{4,6},{5,7},{8,10},{9,11},{12,14},{13,15},{16,18},{17,... | collective-permute-start | bytes 12296 | tf_op jit(solution)/shard_map/ppermute | solution.py:30
  6.6 0.9 broadcast_select_fusion
  7.6 1.6 %collective-permute-start.7 = (f32[2,32,1]{2,1,0:T(8,128)S(1)}, f32[2,32,1]{2,1,0:T(8,128)S(1)}, u32[]{:S(2)}, u32[]{:S(2)}) collective-permute-start(f32[2,32,1]{2,1,0:T(8,128)S(1)} %slice.136), channel_id=1, source_target_pairs={{0,1},{2,3},{4,5},{6,7},{8,9},{10,11},{12,13},{14,15},{16,17},{18,... | collective-permute-start | bytes 776 | tf_op jit(solution)/shard_map/ppermute | solution.py:30
  9.2 1.6 %collective-permute-start.2 = (f32[3,1,32,512]{3,2,1,0:T(8,128)S(1)}, f32[3,1,32,512]{3,2,1,0:T(8,128)S(1)}, u32[]{:S(2)}, u32[]{:S(2)}) collective-permute-start(f32[3,1,32,512]{3,2,1,0:T(8,128)S(1)} %get-tuple-element.22), channel_id=1, source_target_pairs={{0,4},{4,8},{8,12},{12,0},{1,5},{5,9},{9,13},{13,1},{2,6},{6,10},{... | collective-permute-start | bytes 589832 | tf_op jit(solution)/shard_map/ppermute | solution.py:16
  10.9 1.6 %collective-permute-start.1 = (f32[1,32,512]{2,1,0:T(8,128)S(1)}, f32[1,32,512]{2,1,0:T(8,128)S(1)}, u32[]{:S(2)}, u32[]{:S(2)}) collective-permute-start(f32[1,32,512]{2,1,0:T(8,128)S(1)} %get-tuple-element.23), channel_id=1, source_target_pairs={{0,4},{4,8},{8,12},{12,0},{1,5},{5,9},{9,13},{13,1},{2,6},{6,10},{... | collective-permute-start | bytes 196616 | tf_op jit(solution)/shard_map/ppermute | solution.py:24
  12.5 2.2 %collective-permute-start = (f32[3,1,32,512]{3,2,1,0:T(8,128)S(1)}, f32[3,1,32,512]{3,2,1,0:T(8,128)S(1)}, u32[]{:S(2)}, u32[]{:S(2)}) collective-permute-start(f32[3,1,32,512]{3,2,1,0:T(8,128)S(1)} %get-tuple-element.21), channel_id=1, source_target_pairs={{4,0},{8,4},{12,8},{0,12},{5,1},{9,5},{13,9},{1,13},{6,2},{10,6},{... | collective-permute-start | bytes 589832 | tf_op jit(solution)/shard_map/ppermute | solution.py:17
  14.8 4.1 %collective-permute-done.2 = f32[3,1,32,512]{3,2,1,0:T(8,128)S(1)} collective-permute-done((f32[3,1,32,512]{3,2,1,0:T(8,128)S(1)}, f32[3,1,32,512]{3,2,1,0:T(8,128)S(1)}, u32[]{:S(2)}, u32[]{:S(2)}) %collective-permute-start.2) | collective-permute-done | bytes 196640 | tf_op jit(solution)/shard_map/ppermute | solution.py:16
  19.0 3.9 %collective-permute-done = f32[3,1,32,512]{3,2,1,0:T(8,128)S(1)} collective-permute-done((f32[3,1,32,512]{3,2,1,0:T(8,128)S(1)}, f32[3,1,32,512]{3,2,1,0:T(8,128)S(1)}, u32[]{:S(2)}, u32[]{:S(2)}) %collective-permute-start) | collective-permute-done | bytes 196640 | tf_op jit(solution)/shard_map/ppermute | solution.py:17
  23.1 2.0 %collective-permute-start.3 = (f32[3,4,1,512]{3,2,1,0:T(1,128)S(1)}, f32[3,4,1,512]{3,2,1,0:T(1,128)S(1)}, u32[]{:S(2)}, u32[]{:S(2)}) collective-permute-start(f32[3,4,1,512]{3,2,1,0:T(1,128)S(1)} %get-tuple-element.16), channel_id=1, source_target_pairs={{2,0},{0,2},{3,1},{1,3},{6,4},{4,6},{7,5},{5,7},{10,8},{8,10},{11,... | collective-permute-start | bytes 73736 | tf_op jit(solution)/shard_map/ppermute | solution.py:17
  25.1 1.8 %collective-permute-done.5 = f32[3,4,1,512]{3,2,1,0:T(1,128)S(1)} collective-permute-done((f32[3,4,1,512]{3,2,1,0:T(1,128)S(1)}, f32[3,4,1,512]{3,2,1,0:T(1,128)S(1)}, u32[]{:S(2)}, u32[]{:S(2)}) %collective-permute-start.5) | collective-permute-done | bytes 24608 | tf_op jit(solution)/shard_map/ppermute | solution.py:16
  26.9 0.3 collective-permute-done.3
  27.2 0.2 pad_maximum_fusion.35
  27.4 0.5 collective-permute-start.8
  27.9 1.0 collective-permute-done.6
  28.9 0.4 collective-permute-done.8
  29.3 0.6 multiply_reduce_fusion.2
  29.9 32.1 %all-reduce = (f32[3]{0:T(128)S(1)}, f32[3]{0:T(128)S(1)}) all-reduce(f32[3]{0:T(128)S(1)} %get-tuple-element.3, f32[3]{0:T(128)S(1)} %get-tuple-element.2), channel_id=1, replica_groups=mesh['clip'=2,'tm'=4,'row'=2,'col'=2] {'tm','row','col'}, use_global_device_ids=true, to_apply=%region_1.2 | all-reduce | flops 6 | bytes 48 | tf_op jit(solution)/shard_map/psum | solution.py:66
  62.0 0.2 multiply_reduce_fusion.1
  62.2 29.7 %psum.30 = f32[3]{0:T(128)S(1)} all-reduce(f32[3]{0:T(128)S(1)} %multiply_reduce_fusion.1), channel_id=1, replica_groups=mesh['clip'=2,'tm'=4,'row'=2,'col'=2] {'tm','row','col'}, use_global_device_ids=true, to_apply=%region_5.6 | all-reduce | flops 3 | bytes 24 | tf_op jit(solution)/shard_map/psum | solution.py:66
  92.2 3.8 %collective-permute-start.9 = (f32[3,1,32,512]{3,2,1,0:T(8,128)S(1)}, f32[3,1,32,512]{3,2,1,0:T(8,128)S(1)}, u32[]{:S(2)}, u32[]{:S(2)}) collective-permute-start(f32[3,1,32,512]{3,2,1,0:T(8,128)S(1)} %get-tuple-element.20), channel_id=1, source_target_pairs={{4,0},{8,4},{12,8},{0,12},{5,1},{9,5},{13,9},{1,13},{6,2},{10,6},{... | collective-permute-start | bytes 589832 | tf_op jit(solution)/shard_map/ppermute | solution.py:17
  96.0 5.8 %collective-permute-done.10 = f32[3,1,32,512]{3,2,1,0:T(8,128)S(1)} collective-permute-done((f32[3,1,32,512]{3,2,1,0:T(8,128)S(1)}, f32[3,1,32,512]{3,2,1,0:T(8,128)S(1)}, u32[]{:S(2)}, u32[]{:S(2)}) %collective-permute-start.10) | collective-permute-done | bytes 196640 | tf_op jit(solution)/shard_map/ppermute | solution.py:16
  101.8 1.2 collective-permute-done.9
  103.1 2.0 %collective-permute-start.11 = (f32[3,4,1,512]{3,2,1,0:T(1,128)S(1)}, f32[3,4,1,512]{3,2,1,0:T(1,128)S(1)}, u32[]{:S(2)}, u32[]{:S(2)}) collective-permute-start(f32[3,4,1,512]{3,2,1,0:T(1,128)S(1)} %get-tuple-element.14), channel_id=1, source_target_pairs={{2,0},{0,2},{3,1},{1,3},{6,4},{4,6},{7,5},{5,7},{10,8},{8,10},{11,... | collective-permute-start | bytes 73736 | tf_op jit(solution)/shard_map/ppermute | solution.py:17
  105.1 1.8 %collective-permute-done.12 = f32[3,4,1,512]{3,2,1,0:T(1,128)S(1)} collective-permute-done((f32[3,4,1,512]{3,2,1,0:T(1,128)S(1)}, f32[3,4,1,512]{3,2,1,0:T(1,128)S(1)}, u32[]{:S(2)}, u32[]{:S(2)}) %collective-permute-start.12) | collective-permute-done | bytes 24608 | tf_op jit(solution)/shard_map/ppermute | solution.py:16
  106.9 0.3 collective-permute-done.11
  107.4 0.5 collective-permute-start.14
  107.9 1.0 collective-permute-done.13
  108.9 0.4 collective-permute-done.14
  109.3 0.6 multiply_reduce_fusion
  109.9 32.4 %psum.31 = f32[3]{0:T(128)S(1)} all-reduce(f32[3]{0:T(128)S(1)} %get-tuple-element.6), channel_id=1, replica_groups=mesh['clip'=2,'tm'=4,'row'=2,'col'=2] {'tm','row','col'}, use_global_device_ids=true, to_apply=%region_7.8 | all-reduce | flops 3 | bytes 24 | tf_op jit(solution)/shard_map/psum | solution.py:90
  142.3 1.2 multiply_subtract_fusion
  (34 shorter events, 1.1 us)
Async XLA Ops:
  0.6 8.5 %copy-start = (f32[3,2,32,512]{3,2,1,0:T(8,128)S(1)}, f32[3,2,32,512]{3,2,1,0:T(8,128)}, u32[]{:S(2)}) copy-start(f32[3,2,32,512]{3,2,1,0:T(8,128)} %param.5) | copy-start | bytes 1179652
  1.7 23.4 %collective-permute-start.4 = (f32[2,1,512]{2,1,0:T(1,128)S(1)}, f32[2,1,512]{2,1,0:T(1,128)S(1)}, u32[]{:S(2)}, u32[]{:S(2)}) collective-permute-start(f32[2,1,512]{2,1,0:T(1,128)S(1)} %slice.133), channel_id=1, source_target_pairs={{0,2},{1,3},{4,6},{5,7},{8,10},{9,11},{12,14},{13,15},{16,18},{17,... | collective-permute-start | bytes 12296 | tf_op jit(solution)/shard_map/ppermute | solution.py:30
  7.6 3.3 %copy-start.1 = (f32[2,32,512]{2,1,0:T(8,128)S(1)}, f32[2,32,512]{2,1,0:T(8,128)}, u32[]{:S(2)}) copy-start(f32[2,32,512]{2,1,0:T(8,128)} %param.7) | copy-start | bytes 393220
  7.6 7.2 %collective-permute-start.7 = (f32[2,32,1]{2,1,0:T(8,128)S(1)}, f32[2,32,1]{2,1,0:T(8,128)S(1)}, u32[]{:S(2)}, u32[]{:S(2)}) collective-permute-start(f32[2,32,1]{2,1,0:T(8,128)S(1)} %slice.136), channel_id=1, source_target_pairs={{0,1},{2,3},{4,5},{6,7},{8,9},{10,11},{12,13},{14,15},{16,17},{18,... | collective-permute-start | bytes 776 | tf_op jit(solution)/shard_map/ppermute | solution.py:30
  9.2 9.7 %collective-permute-start.2 = (f32[3,1,32,512]{3,2,1,0:T(8,128)S(1)}, f32[3,1,32,512]{3,2,1,0:T(8,128)S(1)}, u32[]{:S(2)}, u32[]{:S(2)}) collective-permute-start(f32[3,1,32,512]{3,2,1,0:T(8,128)S(1)} %get-tuple-element.22), channel_id=1, source_target_pairs={{0,4},{4,8},{8,12},{12,0},{1,5},{5,9},{9,13},{13,1},{2,6},{6,10},{... | collective-permute-start | bytes 589832 | tf_op jit(solution)/shard_map/ppermute | solution.py:16
  10.9 17.0 %collective-permute-start.1 = (f32[1,32,512]{2,1,0:T(8,128)S(1)}, f32[1,32,512]{2,1,0:T(8,128)S(1)}, u32[]{:S(2)}, u32[]{:S(2)}) collective-permute-start(f32[1,32,512]{2,1,0:T(8,128)S(1)} %get-tuple-element.23), channel_id=1, source_target_pairs={{0,4},{4,8},{8,12},{12,0},{1,5},{5,9},{9,13},{13,1},{2,6},{6,10},{... | collective-permute-start | bytes 196616 | tf_op jit(solution)/shard_map/ppermute | solution.py:24
  12.5 10.4 %collective-permute-start = (f32[3,1,32,512]{3,2,1,0:T(8,128)S(1)}, f32[3,1,32,512]{3,2,1,0:T(8,128)S(1)}, u32[]{:S(2)}, u32[]{:S(2)}) collective-permute-start(f32[3,1,32,512]{3,2,1,0:T(8,128)S(1)} %get-tuple-element.21), channel_id=1, source_target_pairs={{4,0},{8,4},{12,8},{0,12},{5,1},{9,5},{13,9},{1,13},{6,2},{10,6},{... | collective-permute-start | bytes 589832 | tf_op jit(solution)/shard_map/ppermute | solution.py:17
  23.0 3.9 %collective-permute-start.5 = (f32[3,4,1,512]{3,2,1,0:T(1,128)S(1)}, f32[3,4,1,512]{3,2,1,0:T(1,128)S(1)}, u32[]{:S(2)}, u32[]{:S(2)}) collective-permute-start(f32[3,4,1,512]{3,2,1,0:T(1,128)S(1)} %get-tuple-element.15), channel_id=1, source_target_pairs={{0,2},{2,0},{1,3},{3,1},{4,6},{6,4},{5,7},{7,5},{8,10},{10,8},{9,1... | collective-permute-start | bytes 73736 | tf_op jit(solution)/shard_map/ppermute | solution.py:16
  23.1 4.1 %collective-permute-start.3 = (f32[3,4,1,512]{3,2,1,0:T(1,128)S(1)}, f32[3,4,1,512]{3,2,1,0:T(1,128)S(1)}, u32[]{:S(2)}, u32[]{:S(2)}) collective-permute-start(f32[3,4,1,512]{3,2,1,0:T(1,128)S(1)} %get-tuple-element.16), channel_id=1, source_target_pairs={{2,0},{0,2},{3,1},{1,3},{6,4},{4,6},{7,5},{5,7},{10,8},{8,10},{11,... | collective-permute-start | bytes 73736 | tf_op jit(solution)/shard_map/ppermute | solution.py:17
  27.3 1.6 %collective-permute-start.6 = (f32[3,4,34,1]{3,2,1,0:T(8,128)S(1)}, f32[3,4,34,1]{3,2,1,0:T(8,128)S(1)}, u32[]{:S(2)}, u32[]{:S(2)}) collective-permute-start(f32[3,4,34,1]{3,2,1,0:T(8,128)S(1)} %get-tuple-element.11), channel_id=1, source_target_pairs={{1,0},{0,1},{3,2},{2,3},{5,4},{4,5},{7,6},{6,7},{9,8},{8,9},{11,10... | collective-permute-start | bytes 4904 | tf_op jit(solution)/shard_map/ppermute | solution.py:17
  27.4 1.9 %collective-permute-start.8 = (f32[3,4,34,1]{3,2,1,0:T(8,128)S(1)}, f32[3,4,34,1]{3,2,1,0:T(8,128)S(1)}, u32[]{:S(2)}, u32[]{:S(2)}) collective-permute-start(f32[3,4,34,1]{3,2,1,0:T(8,128)S(1)} %get-tuple-element.12), channel_id=1, source_target_pairs={{0,1},{1,0},{2,3},{3,2},{4,5},{5,4},{6,7},{7,6},{8,9},{9,8},{10,11... | collective-permute-start | bytes 4904 | tf_op jit(solution)/shard_map/ppermute | solution.py:16
  27.9 1.4 copy-start.2
  92.1 9.7 %collective-permute-start.10 = (f32[3,1,32,512]{3,2,1,0:T(8,128)S(1)}, f32[3,1,32,512]{3,2,1,0:T(8,128)S(1)}, u32[]{:S(2)}, u32[]{:S(2)}) collective-permute-start(f32[3,1,32,512]{3,2,1,0:T(8,128)S(1)} %get-tuple-element.19), channel_id=1, source_target_pairs={{0,4},{4,8},{8,12},{12,0},{1,5},{5,9},{9,13},{13,1},{2,6},{6,10},{... | collective-permute-start | bytes 589832 | tf_op jit(solution)/shard_map/ppermute | solution.py:16
  92.2 10.8 %collective-permute-start.9 = (f32[3,1,32,512]{3,2,1,0:T(8,128)S(1)}, f32[3,1,32,512]{3,2,1,0:T(8,128)S(1)}, u32[]{:S(2)}, u32[]{:S(2)}) collective-permute-start(f32[3,1,32,512]{3,2,1,0:T(8,128)S(1)} %get-tuple-element.20), channel_id=1, source_target_pairs={{4,0},{8,4},{12,8},{0,12},{5,1},{9,5},{13,9},{1,13},{6,2},{10,6},{... | collective-permute-start | bytes 589832 | tf_op jit(solution)/shard_map/ppermute | solution.py:17
  103.0 3.9 %collective-permute-start.12 = (f32[3,4,1,512]{3,2,1,0:T(1,128)S(1)}, f32[3,4,1,512]{3,2,1,0:T(1,128)S(1)}, u32[]{:S(2)}, u32[]{:S(2)}) collective-permute-start(f32[3,4,1,512]{3,2,1,0:T(1,128)S(1)} %get-tuple-element.13), channel_id=1, source_target_pairs={{0,2},{2,0},{1,3},{3,1},{4,6},{6,4},{5,7},{7,5},{8,10},{10,8},{9,1... | collective-permute-start | bytes 73736 | tf_op jit(solution)/shard_map/ppermute | solution.py:16
  103.1 4.1 %collective-permute-start.11 = (f32[3,4,1,512]{3,2,1,0:T(1,128)S(1)}, f32[3,4,1,512]{3,2,1,0:T(1,128)S(1)}, u32[]{:S(2)}, u32[]{:S(2)}) collective-permute-start(f32[3,4,1,512]{3,2,1,0:T(1,128)S(1)} %get-tuple-element.14), channel_id=1, source_target_pairs={{2,0},{0,2},{3,1},{1,3},{6,4},{4,6},{7,5},{5,7},{10,8},{8,10},{11,... | collective-permute-start | bytes 73736 | tf_op jit(solution)/shard_map/ppermute | solution.py:17
  107.4 1.6 %collective-permute-start.13 = (f32[3,4,34,1]{3,2,1,0:T(8,128)S(1)}, f32[3,4,34,1]{3,2,1,0:T(8,128)S(1)}, u32[]{:S(2)}, u32[]{:S(2)}) collective-permute-start(f32[3,4,34,1]{3,2,1,0:T(8,128)S(1)} %get-tuple-element.9), channel_id=1, source_target_pairs={{1,0},{0,1},{3,2},{2,3},{5,4},{4,5},{7,6},{6,7},{9,8},{8,9},{11,10... | collective-permute-start | bytes 4904 | tf_op jit(solution)/shard_map/ppermute | solution.py:17
  107.4 1.9 %collective-permute-start.14 = (f32[3,4,34,1]{3,2,1,0:T(8,128)S(1)}, f32[3,4,34,1]{3,2,1,0:T(8,128)S(1)}, u32[]{:S(2)}, u32[]{:S(2)}) collective-permute-start(f32[3,4,34,1]{3,2,1,0:T(8,128)S(1)} %get-tuple-element.10), channel_id=1, source_target_pairs={{0,1},{1,0},{2,3},{3,2},{4,5},{5,4},{6,7},{7,6},{8,9},{9,8},{10,11... | collective-permute-start | bytes 4904 | tf_op jit(solution)/shard_map/ppermute | solution.py:16
where the time goes:
time: 144 us; the launch traced here: 143 us
  blocking collectives  94.2 us (65%)
  waiting for transfers between devices  21.9 us (15%)
  starting transfers between devices  21.1 us (15%)
  other arithmetic  5.21 us (4%)
    psum x2, blocking collectives, squares(): return lax.psum(channel_sum(residual, residual), ('tm', 'row', 'col'))  61.8 us
    psum x1, blocking collectives, shards(): product = lax.psum(channel_sum(direction, image), ('tm', 'row', 'col'))  32.4 us
    ppermute x6, waiting for transfers between devices, padded_2(): before = lax.ppermute(last, axis, up)  14.2 us
    ppermute x6, starting transfers between devices, padded_2(): after = lax.ppermute(leading, axis, down)  10.2 us
    ppermute x6, waiting for transfers between devices, padded_2(): after = lax.ppermute(leading, axis, down)  7.68 us
    ppermute x2, starting transfers between devices, passed_along(): return lax.ppermute(block, axis, route)  6.43 us
  transfers between devices with their start and end apart: 15, of which 12 were waited for; matrix products, arithmetic and copies ran while one was open for 1% of the time, Pallas kernels for 0%

commit v1 on v0

v1 whole, which is shorter than its diff:
```python
import functools

import jax
import jax.numpy as jnp
from jax import lax
from jax.experimental import pallas as pl
from jax.experimental.pallas import tpu as pltpu
from jax.sharding import PartitionSpec as P

MESH = pl.DeviceIdType.MESH
LANES = 128


def kernel(sizes, b, s, wt, wy, wx, x_out, r_out,
           bv, sv, wtv, wyv, wxv, byv, bxv, av, rv, pv, qv,
           hz, hwt, srow, hrow, hcol, hwx, xo, ro, part1, part2,
           load_sem, z_send, z_recv, wt_send, wt_recv, row_send, row_recv,
           col_send, col_recv, wx_send, wx_recv, sum1_send, sum1_recv,
           sum2_send, sum2_recv, out_sem):
    tms, bands, strips = sizes
    chans, frames, rows, cols = b.shape
    me_t, me_r, me_c = (lax.axis_index(a) for a in ("tm", "row", "col"))
    up_t, down_t = lax.rem(me_t + 1, tms), lax.rem(me_t + tms - 1, tms)
    up_r, down_r = lax.rem(me_r + 1, bands), lax.rem(me_r + bands - 1, bands)
    up_c, down_c = lax.rem(me_c + 1, strips), lax.rem(me_c + strips - 1, strips)
    sends = []

    def send(src, dst, ss, rs, **where):
        copy = pltpu.make_async_remote_copy(
            src_ref=src, dst_ref=dst, send_sem=ss, recv_sem=rs,
            device_id=where, device_id_type=MESH)
        copy.start()
        sends.append(copy)
        return copy

    loads = [pltpu.make_async_copy(h, v, load_sem.at[i]) for i, (h, v) in enumerate(
        ((b, bv), (wy, wyv), (wx, wxv), (s, sv), (wt, wtv)))]
    for copy in loads:
        copy.start()

    group = [(i, j) for i in range(bands) for j in range(strips) if i or j]
    barrier = pltpu.get_barrier_semaphore()
    for d in range(1, tms):
        pl.semaphore_signal(barrier, inc=1, device_id={"tm": lax.rem(me_t + d, tms)}, device_id_type=MESH)
    for i, j in group:
        pl.semaphore_signal(barrier, inc=1, device_id={
            "row": lax.rem(me_r + i, bands), "col": lax.rem(me_c + j, strips)}, device_id_type=MESH)
    pl.semaphore_wait(barrier, tms - 1 + len(group))

    def send_time(phase, c, field):
        up = send(field.at[c, frames - 1], hz.at[phase, 0, c], z_send.at[phase, 0, c], z_recv.at[phase, 0, c], tm=up_t)
        down = send(field.at[c, 0], hz.at[phase, 1, c], z_send.at[phase, 1, c], z_recv.at[phase, 1, c], tm=down_t)
        return [up, down]

    def send_side(phase, c, field):
        for f in range(frames):
            srow[phase, 0, c, f:f + 1, :] = field[c, f, rows - 1:rows, :]
            srow[phase, 1, c, f:f + 1, :] = field[c, f, 0:1, :]
            if phase == 0 and c == 0:
                srow[phase, 0, c, frames + f:frames + f + 1, :] = wyv[f, rows - 1:rows, :]
        return [
            send(srow.at[phase, 0, c], hrow.at[phase, 0, c], row_send.at[phase, 0, c], row_recv.at[phase, 0, c], row=up_r),
            send(srow.at[phase, 1, c], hrow.at[phase, 1, c], row_send.at[phase, 1, c], row_recv.at[phase, 1, c], row=down_r),
            send(field.at[c, :, :, cols - LANES:], hcol.at[phase, 0, c], col_send.at[phase, 0, c], col_recv.at[phase, 0, c], col=up_c),
            send(field.at[c, :, :, :LANES], hcol.at[phase, 1, c], col_send.at[phase, 1, c], col_recv.at[phase, 1, c], col=down_c),
        ]

    wait_b = {}
    weight = send(wt.at[frames - 1], hwt, wt_send, wt_recv, tm=up_t)
    for c in range(chans):
        wait_b[c] = send_time(0, c, b)

    row_ids = lax.broadcasted_iota(jnp.int32, (rows, cols), 0)
    lane_ids = lax.broadcasted_iota(jnp.int32, (rows, LANES), 1)
    last_band = me_r == bands - 1
    last_strip = me_c == strips - 1
    for copy in loads[:3]:
        copy.wait()
    for f in range(frames):
        wyv[f, rows - 1:rows, :] = jnp.where(last_band, 0.0, wyv[f, rows - 1:rows, :])
        tile = wxv[f, :, cols - LANES:]
        wxv[f, :, cols - LANES:] = jnp.where(jnp.logical_and(last_strip, lane_ids == LANES - 1), 0.0, tile)
    strip = send(wxv.at[:, :, cols - LANES:], hwx, wx_send, wx_recv, col=up_c)
    for c in range(chans):
        wait_b[c] += send_side(0, c, bv)

    def before_row(value, rim):
        return jnp.where(row_ids == 0, rim, pltpu.roll(value, 1, 0))

    def after_row(value, rim):
        return jnp.where(row_ids == rows - 1, rim, pltpu.roll(value, rows - 1, 0))

    def before_col(value, rim):
        moved = pltpu.roll(value, 1, 1)
        edge = jnp.where(lane_ids == 0, pltpu.roll(rim, 1, 1), moved[:, :LANES])
        return jnp.concatenate([edge, moved[:, LANES:]], axis=1)

    def after_col(value, rim):
        moved = pltpu.roll(value, cols - 1, 1)
        edge = jnp.where(lane_ids == LANES - 1, pltpu.roll(rim, LANES - 1, 1), moved[:, cols - LANES:])
        return jnp.concatenate([moved[:, :cols - LANES], edge], axis=1)

    def operate(c, f, field, rim):
        v = field[c, f]
        after = field[c, f + 1] if f < frames - 1 else rim(hz, 1, c)
        prior = field[c, f - 1] if f > 0 else rim(hz, 0, c)
        before_time = wtv[f - 1] if f > 0 else hwt[...]
        one = slice(f, f + 1)
        total = sv[f] * v
        total = total + wtv[f] * (v - after)
        total = total + before_time * (v - prior)
        total = total + wyv[f] * (v - after_row(v, rim(hrow, 1, c, one)))
        total = total + byv[f] * (v - before_row(v, rim(hrow, 0, c, one)))
        total = total + wxv[f] * (v - after_col(v, rim(hcol, 1, c, f)))
        total = total + bxv[f] * (v - before_col(v, rim(hcol, 0, c, f)))
        return total

    tile_rows = lax.broadcasted_iota(jnp.int32, (8, LANES), 0)

    def lanes_sum(value):
        value = jnp.sum(value, axis=0, keepdims=True)
        total = value[:, :LANES]
        for k in range(LANES, cols, LANES):
            total = total + value[:, k:k + LANES]
        return total

    def total_of(k, parts):
        tile = jnp.zeros((8, LANES), jnp.float32)
        for q, value in enumerate(parts):
            tile = jnp.where(tile_rows == q, value, tile)
        mine = me_r * strips + me_c
        part1[k, mine] = tile
        for n, (i, j) in enumerate(group):
            to_r, to_c = lax.rem(me_r + i, bands), lax.rem(me_c + j, strips)
            send(part1.at[k, mine], part1.at[k, mine], sum1_send.at[k, n], sum1_recv.at[k, mine], row=to_r, col=to_c)
        for i, j in group:
            other = lax.rem(me_r + i, bands) * strips + lax.rem(me_c + j, strips)
            pltpu.make_async_copy(part1.at[k, other], part1.at[k, other], sum1_recv.at[k, other]).wait()
        tile = part1[k, 0]
        for n in range(1, bands * strips):
            tile = tile + part1[k, n]
        part2[k, me_t] = tile
        for d in range(1, tms):
            send(part2.at[k, me_t], part2.at[k, me_t], sum2_send.at[k, d], sum2_recv.at[k, me_t], tm=lax.rem(me_t + d, tms))
        for d in range(1, tms):
            other = lax.rem(me_t + d, tms)
            pltpu.make_async_copy(part2.at[k, other], part2.at[k, other], sum2_recv.at[k, other]).wait()
        tile = part2[k, 0]
        for n in range(1, tms):
            tile = tile + part2[k, n]
        return jnp.sum(tile, axis=1, keepdims=True)

    def plain(ref, *index):
        return ref[(0,) + index]

    for copy in loads[3:]:
        copy.wait()
    weight.wait_recv()
    strip.wait_recv()
    wait_a, squares, products = {}, [], []
    for c in range(chans):
        for copy in wait_b[c]:
            copy.wait_recv()
        if c == 0:
            for f in range(frames):
                byv[f] = before_row(wyv[f], hrow[0, 0, 0, frames + f:frames + f + 1])
                bxv[f] = before_col(wxv[f], hwx[f])
        square, product = 0.0, 0.0
        for f in range(frames):
            image = operate(c, f, bv, plain)
            av[c, f] = image
            square = square + bv[c, f] * bv[c, f]
            product = product + bv[c, f] * image
        wait_a[c] = send_time(1, c, av) + send_side(1, c, av)
        squares.append(lanes_sum(square))
        products.append(lanes_sum(product))

    sums = total_of(0, squares + products)
    norm0 = [sums[c:c + 1] for c in range(chans)]
    alpha0 = [sums[c:c + 1] / sums[chans + c:chans + c + 1] for c in range(chans)]
    squares = []
    for c in range(chans):
        square = 0.0
        for f in range(frames):
            residual = bv[c, f] - alpha0[c] * av[c, f]
            rv[c, f] = residual
            square = square + residual * residual
        squares.append(lanes_sum(square))
    sums = total_of(1, squares)
    norm1 = [sums[c:c + 1] for c in range(chans)]
    beta = [norm1[c] / norm0[c] for c in range(chans)]

    def combined(ref, side, c, *index):
        own = ref[(0, side, c) + index]
        return (own - alpha0[c] * ref[(1, side, c) + index]) + beta[c] * own

    for c in range(chans):
        for f in range(frames):
            pv[c, f] = rv[c, f] + beta[c] * bv[c, f]
    products = []
    for c in range(chans):
        for copy in wait_a[c]:
            copy.wait_recv()
        product = 0.0
        for f in range(frames):
            image = operate(c, f, pv, combined)
            qv[c, f] = image
            product = product + pv[c, f] * image
        products.append(lanes_sum(product))
    sums = total_of(2, products)
    outs = []
    for c in range(chans):
        alpha1 = norm1[c] / sums[c:c + 1]
        for f in range(frames):
            xo[c, f] = alpha0[c] * bv[c, f] + alpha1 * pv[c, f]
            ro[c, f] = rv[c, f] - alpha1 * qv[c, f]
        for i, (v, h) in enumerate(((xo, x_out), (ro, r_out))):
            copy = pltpu.make_async_copy(v.at[c], h.at[c], out_sem.at[i, c])
            copy.start()
            outs.append(copy)
    for copy in sends:
        copy.wait_send()
    for copy in outs:
        copy.wait()


def shards(sizes, right_side, screening, time_weight, row_weight, column_weight):
    tms, bands, strips = sizes
    chans, frames, rows, cols = right_side.shape
    f32 = jnp.float32
    field = pltpu.VMEM((chans, frames, rows, cols), f32)
    coefficient = pltpu.VMEM((frames, rows, cols), f32)
    tall = -(-2 * frames // 8) * 8
    dma = pltpu.SemaphoreType.DMA
    anywhere = pl.BlockSpec(memory_space=pl.ANY)
    shape = jax.ShapeDtypeStruct(right_side.shape, f32)
    return pl.pallas_call(
        functools.partial(kernel, sizes),
        out_shape=(shape, shape),
        in_specs=[anywhere] * 5,
        out_specs=(anywhere, anywhere),
        scratch_shapes=[field] + [coefficient] * 6 + [field] * 4 + [
            pltpu.VMEM((2, 2, chans, rows, cols), f32),
            pltpu.VMEM((rows, cols), f32),
            pltpu.VMEM((2, 2, chans, tall, cols), f32),
            pltpu.VMEM((2, 2, chans, tall, cols), f32),
            pltpu.VMEM((2, 2, chans, frames, rows, LANES), f32),
            pltpu.VMEM((frames, rows, LANES), f32),
            field, field,
            pltpu.VMEM((3, bands * strips, 8, LANES), f32),
            pltpu.VMEM((3, tms, 8, LANES), f32),
            dma((5,)),
            dma((2, 2, chans)), dma((2, 2, chans)), dma, dma,
            dma((2, 2, chans)), dma((2, 2, chans)),
            dma((2, 2, chans)), dma((2, 2, chans)), dma, dma,
            dma((3, bands * strips)), dma((3, bands * strips)),
            dma((3, tms)), dma((3, tms)),
            dma((2, chans)),
        ],
        compiler_params=pltpu.CompilerParams(
            collective_id=0, has_side_effects=True, vmem_limit_bytes=24 * 1024 * 1024),
        cost_estimate=pl.CostEstimate(flops=10_000_000, bytes_accessed=2_000_000, transcendentals=0),
    )(right_side, screening, time_weight, row_weight, column_weight)


def solution(mesh):
    field = P(None, ("clip", "tm"), "row", "col")
    coefficient = P(("clip", "tm"), "row", "col")
    sizes = tuple(mesh.shape[a] for a in ("tm", "row", "col"))
    return jax.shard_map(
        functools.partial(shards, sizes),
        mesh=mesh,
        in_specs=(field,) + (coefficient,) * 4,
        out_specs=(field, field),
        check_vma=False,
    )
```

time: 144 us -> 49.8 us (0.35)
  blocking collectives: 94.2 us -> 0 us
  Pallas kernels: 0 us -> 42.8 us
  waiting for transfers between devices: 21.9 us -> 0 us
  starting transfers between devices: 21.1 us -> 0 us
  local copies, waits for them, and re-layouts: 0.25 us -> 6.1 us
  other arithmetic: 5.21 us -> 0 us
    psum x3 -> x0, blocking collectives: 94.2 us -> none  [the longest x2 61.8 us: squares(): return lax.psum(channel_sum(residual, residual), ('tm', 'row', 'col'))]
    pallas_call x0 -> x1, Pallas kernels: none -> 42.8 us  [shards(): pl.pallas_call(functools.partial(kernel, sizes), out_shape=(shape, shape)...]
    ppermute x15 -> x0, waiting for transfers between devices: 21.9 us -> none  [the longest x6 14.2 us: padded_2(): before = lax.ppermute(last, axis, up)]
    ppermute x15 -> x0, starting transfers between devices: 21.1 us -> none  [the longest x6 10.2 us: padded_2(): after = lax.ppermute(leading, axis, down)]
    unnamed x8 -> x12, local copies, waits for them, and re-layouts: 0.05 us -> 6.1 us
    select_n x2 -> x0, other arithmetic: 1.95 us -> none  [the longest x1 1.03 us: shards(): jnp.where(jnp.logical_and(last_band, row_ids == rows - 1), 0.0, row_weight)]
  transfers between devices with their start and end apart: 15 -> 0, of which waited for: 12 -> 0; matrix products, arithmetic and copies ran while one was open for 1% -> 0% of each run, Pallas kernels for 0% -> 0%
where the time goes in v1:
time: 49.8 us; the launch traced here: 49.6 us
  Pallas kernels  42.8 us (86%)
  local copies, waits for them, and re-layouts  6.1 us (12%)
  between operations  0.65 us (1%)
    pallas_call x1, Pallas kernels, shards(): pl.pallas_call(functools.partial(kernel, sizes), out_shape=(shape, shape)...  42.8 us
    unnamed x12, local copies, waits for them, and re-layouts  6.1 us

profile of v1, /device:TPU:0, one launch (start us, length us, event | category | flops | bytes accessed | tf_op | source)
XLA Modules:
  0.0 49.6 jit_solution(4536443464214836960)
XLA Ops:
  0.6 0.0 copy-start
  0.6 1.0 %copy-done = f32[3,2,32,512]{3,2,1,0:T(8,128)S(1)} copy-done((f32[3,2,32,512]{3,2,1,0:T(8,128)S(1)}, f32[3,2,32,512]{3,2,1,0:T(8,128)}, u32[]{:S(2)}) %copy-start) | copy-done | bytes 393240
  1.6 0.0 copy-start.1
  1.6 0.9 %copy-done.1 = f32[2,32,512]{2,1,0:T(8,128)S(1)} copy-done((f32[2,32,512]{2,1,0:T(8,128)S(1)}, f32[2,32,512]{2,1,0:T(8,128)}, u32[]{:S(2)}) %copy-start.1) | copy-done | bytes 131096
  2.5 0.0 copy-start.2
  2.5 0.9 %copy-done.2 = f32[2,32,512]{2,1,0:T(8,128)S(1)} copy-done((f32[2,32,512]{2,1,0:T(8,128)S(1)}, f32[2,32,512]{2,1,0:T(8,128)}, u32[]{:S(2)}) %copy-start.2) | copy-done | bytes 131096
  3.4 0.0 copy-start.3
  3.4 0.9 %copy-done.3 = f32[2,32,512]{2,1,0:T(8,128)S(1)} copy-done((f32[2,32,512]{2,1,0:T(8,128)S(1)}, f32[2,32,512]{2,1,0:T(8,128)}, u32[]{:S(2)}) %copy-start.3) | copy-done | bytes 131096
  4.3 0.0 copy-start.4
  4.3 0.9 %copy-done.4 = f32[2,32,512]{2,1,0:T(8,128)S(1)} copy-done((f32[2,32,512]{2,1,0:T(8,128)S(1)}, f32[2,32,512]{2,1,0:T(8,128)}, u32[]{:S(2)}) %copy-start.4) | copy-done | bytes 131096
  5.2 42.8 %shard_map.68 = (f32[3,2,32,512]{3,2,1,0:T(8,128)S(1)}, f32[3,2,32,512]{3,2,1,0:T(8,128)S(1)}) custom-call(f32[3,2,32,512]{3,2,1,0:T(8,128)S(1)} %copy-done, f32[2,32,512]{2,1,0:T(8,128)S(1)} %copy-done.1, f32[2,32,512]{2,1,0:T(8,128)S(1)} %copy-done.2, f32[2,32,512]{2,1,0:T(8,128)S(1)} %copy-done.3, f32[2,32,512]{2,1,0:T(8,128)S(1)} %copy-done.4), custom_call_target="tpu_custom_call" | custom-call | flops 10000000 | bytes 2000000 | tf_op jit(solution)/shard_map/pallas_call | solution.py:237
  48.1 0.7 %copy.9 = f32[3,2,32,512]{3,2,1,0:T(8,128)} copy(f32[3,2,32,512]{3,2,1,0:T(8,128)S(1)} %get-tuple-element.4) | data formatting | bytes 786432
  48.8 0.7 %copy.10 = f32[3,2,32,512]{3,2,1,0:T(8,128)} copy(f32[3,2,32,512]{3,2,1,0:T(8,128)S(1)} %get-tuple-element.5) | data formatting | bytes 786432
Async XLA Ops:
  0.6 1.0 %copy-start = (f32[3,2,32,512]{3,2,1,0:T(8,128)S(1)}, f32[3,2,32,512]{3,2,1,0:T(8,128)}, u32[]{:S(2)}) copy-start(f32[3,2,32,512]{3,2,1,0:T(8,128)} %b.1) | copy-start | bytes 1179652
  1.6 0.9 %copy-start.1 = (f32[2,32,512]{2,1,0:T(8,128)S(1)}, f32[2,32,512]{2,1,0:T(8,128)}, u32[]{:S(2)}) copy-start(f32[2,32,512]{2,1,0:T(8,128)} %s.1) | copy-start | bytes 393220
  2.5 0.9 %copy-start.2 = (f32[2,32,512]{2,1,0:T(8,128)S(1)}, f32[2,32,512]{2,1,0:T(8,128)}, u32[]{:S(2)}) copy-start(f32[2,32,512]{2,1,0:T(8,128)} %wt.1) | copy-start | bytes 393220
  3.4 0.9 %copy-start.3 = (f32[2,32,512]{2,1,0:T(8,128)S(1)}, f32[2,32,512]{2,1,0:T(8,128)}, u32[]{:S(2)}) copy-start(f32[2,32,512]{2,1,0:T(8,128)} %wy.1) | copy-start | bytes 393220
  4.3 0.9 %copy-start.4 = (f32[2,32,512]{2,1,0:T(8,128)S(1)}, f32[2,32,512]{2,1,0:T(8,128)}, u32[]{:S(2)}) copy-start(f32[2,32,512]{2,1,0:T(8,128)} %wx.1) | copy-start | bytes 393220

commit v2 on v1

v2 whole, which is shorter than its diff:
```python
import functools

import jax
import jax.numpy as jnp
from jax import lax
from jax.experimental import pallas as pl
from jax.experimental.pallas import tpu as pltpu
from jax.sharding import PartitionSpec as P

MESH = pl.DeviceIdType.MESH
LANES = 128
VMEM_BYTES = 60 * 1024 * 1024


def kernel(sizes, b, s, wt, wy, wx, x_out, r_out,
           bv, sv, wtv, wyv, wxv, byv, bxv, av, rv, pv, qv,
           hz, hwt, srow, hrow, hcol, hwx, part,
           load_sem, z_send, z_recv, wt_send, wt_recv, row_send, row_recv,
           col_send, col_recv, wx_send, wx_recv, sum_send, sum_recv):
    tms, bands, strips = sizes
    chans, frames, rows, cols = b.shape
    half = rows // 2
    me_t, me_r, me_c = (lax.axis_index(a) for a in ("tm", "row", "col"))
    up_t, down_t = lax.rem(me_t + 1, tms), lax.rem(me_t + tms - 1, tms)
    up_r, down_r = lax.rem(me_r + 1, bands), lax.rem(me_r + bands - 1, bands)
    up_c, down_c = lax.rem(me_c + 1, strips), lax.rem(me_c + strips - 1, strips)
    sends = []

    def send(src, dst, ss, rs, **where):
        copy = pltpu.make_async_remote_copy(
            src_ref=src, dst_ref=dst, send_sem=ss, recv_sem=rs,
            device_id=where, device_id_type=MESH)
        copy.start()
        sends.append(copy)
        return copy

    loads = [pltpu.make_async_copy(h, v, load_sem.at[i]) for i, (h, v) in enumerate(
        ((b, bv), (wy, wyv), (wx, wxv), (s, sv), (wt, wtv)))]
    for copy in loads:
        copy.start()

    group = []
    for t in range(tms):
        for i in range(bands):
            for j in range(strips):
                if t or i or j:
                    where = (lax.rem(me_t + t, tms), lax.rem(me_r + i, bands), lax.rem(me_c + j, strips))
                    group.append((dict(zip(("tm", "row", "col"), where)), (where[0] * bands + where[1]) * strips + where[2]))
    mine = (me_t * bands + me_r) * strips + me_c
    barrier = pltpu.get_barrier_semaphore()
    for where, _ in group:
        pl.semaphore_signal(barrier, inc=1, device_id=where, device_id_type=MESH)
    pl.semaphore_wait(barrier, len(group))

    def send_time(phase, c, field, early):
        n = 1 - early
        fore = pl.ds(n * half, half)
        back = pl.ds((1 - n) * half, half)
        return [
            send(field.at[c, frames - 1, fore], hz.at[phase, 0, c, fore], z_send.at[phase, 0, c, n], z_recv.at[phase, 0, c, n], tm=up_t),
            send(field.at[c, 0, back], hz.at[phase, 1, c, back], z_send.at[phase, 1, c, n], z_recv.at[phase, 1, c, n], tm=down_t),
        ]

    def send_frames(c, field):
        return [
            send(field.at[c, frames - 1], hz.at[0, 0, c], z_send.at[0, 0, c, 0], z_recv.at[0, 0, c, 0], tm=up_t),
            send(field.at[c, 0], hz.at[0, 1, c], z_send.at[0, 1, c, 0], z_recv.at[0, 1, c, 0], tm=down_t),
        ]

    def send_side(phase, c, field):
        for f in range(frames):
            srow[phase, 0, c, f:f + 1, :] = field[c, f, rows - 1:rows, :]
            srow[phase, 1, c, f:f + 1, :] = field[c, f, 0:1, :]
            if phase == 0 and c == 0:
                srow[phase, 0, c, frames + f:frames + f + 1, :] = wyv[f, rows - 1:rows, :]
        return [
            send(srow.at[phase, 0, c], hrow.at[phase, 0, c], row_send.at[phase, 0, c], row_recv.at[phase, 0, c], row=up_r),
            send(srow.at[phase, 1, c], hrow.at[phase, 1, c], row_send.at[phase, 1, c], row_recv.at[phase, 1, c], row=down_r),
            send(field.at[c, :, :, cols - LANES:], hcol.at[phase, 0, c], col_send.at[phase, 0, c], col_recv.at[phase, 0, c], col=up_c),
            send(field.at[c, :, :, :LANES], hcol.at[phase, 1, c], col_send.at[phase, 1, c], col_recv.at[phase, 1, c], col=down_c),
        ]

    wait_b = {}
    weight = send(wt.at[frames - 1], hwt, wt_send, wt_recv, tm=up_t)
    for c in range(chans):
        wait_b[c] = send_frames(c, b)

    row_ids = lax.broadcasted_iota(jnp.int32, (rows, cols), 0)
    lane_ids = lax.broadcasted_iota(jnp.int32, (rows, LANES), 1)
    last_band = me_r == bands - 1
    last_strip = me_c == strips - 1
    for copy in loads[:3]:
        copy.wait()
    for f in range(frames):
        wyv[f, rows - 1:rows, :] = jnp.where(last_band, 0.0, wyv[f, rows - 1:rows, :])
        tile = wxv[f, :, cols - LANES:]
        wxv[f, :, cols - LANES:] = jnp.where(jnp.logical_and(last_strip, lane_ids == LANES - 1), 0.0, tile)
    strip = send(wxv.at[:, :, cols - LANES:], hwx, wx_send, wx_recv, col=up_c)
    for c in range(chans):
        wait_b[c] += send_side(0, c, bv)

    def before_row(value, rim):
        return jnp.where(row_ids == 0, rim, pltpu.roll(value, 1, 0))

    def after_row(value, rim):
        return jnp.where(row_ids == rows - 1, rim, pltpu.roll(value, rows - 1, 0))

    def before_col(value, rim):
        moved = pltpu.roll(value, 1, 1)
        edge = jnp.where(lane_ids == 0, pltpu.roll(rim, 1, 1), moved[:, :LANES])
        return jnp.concatenate([edge, moved[:, LANES:]], axis=1)

    def after_col(value, rim):
        moved = pltpu.roll(value, cols - 1, 1)
        edge = jnp.where(lane_ids == LANES - 1, pltpu.roll(rim, LANES - 1, 1), moved[:, cols - LANES:])
        return jnp.concatenate([moved[:, :cols - LANES], edge], axis=1)

    def inner(c, f, field, rim):
        v = field[c, f]
        one = slice(f, f + 1)
        total = sv[f] * v
        if f < frames - 1:
            total = total + wtv[f] * (v - field[c, f + 1])
        if f > 0:
            total = total + wtv[f - 1] * (v - field[c, f - 1])
        total = total + wyv[f] * (v - after_row(v, rim(hrow, 1, c, one)))
        total = total + byv[f] * (v - before_row(v, rim(hrow, 0, c, one)))
        total = total + wxv[f] * (v - after_col(v, rim(hcol, 1, c, f)))
        total = total + bxv[f] * (v - before_col(v, rim(hcol, 0, c, f)))
        return total

    def outer(c, f, field, rim):
        total = 0.0
        if f == 0:
            total = total + hwt[...] * (field[c, f] - rim(hz, 0, c))
        if f == frames - 1:
            total = total + wtv[f] * (field[c, f] - rim(hz, 1, c))
        return total

    def whole_sum(value):
        return jnp.sum(jnp.sum(value, axis=0, keepdims=True), axis=1, keepdims=True)

    row_lanes = lax.broadcasted_iota(jnp.int32, (1, LANES), 1)

    def exchange(k, values):
        line = jnp.zeros((1, LANES), jnp.float32)
        for (q, c), value in values.items():
            line = jnp.where(row_lanes == 8 * q + c, value, line)
        part[k, mine] = line
        copies = [send(part.at[k, mine], part.at[k, mine], sum_send.at[k, n], sum_recv.at[k, mine], **where)
                  for n, (where, _) in enumerate(group)]
        return copies

    def collect(k):
        for _, other in group:
            pltpu.make_async_copy(part.at[k, other], part.at[k, other], sum_recv.at[k, other]).wait()
        return jnp.concatenate([part[k, n] for n in range(tms * bands * strips)], axis=0)

    def plain(ref, *index):
        return ref[(0,) + index]

    for copy in loads[3:]:
        copy.wait()
    weight.wait_recv()
    strip.wait_recv()
    wait_side, wait_early, wait_late, values = {}, {}, {}, {}
    for c in range(chans):
        for copy in wait_b[c]:
            copy.wait_recv()
        if c == 0:
            for f in range(frames):
                byv[f] = before_row(wyv[f], hrow[0, 0, 0, frames + f:frames + f + 1])
                bxv[f] = before_col(wxv[f], hwx[f])
        m0, m1, m2 = 0.0, 0.0, 0.0
        for f in range(frames):
            image = inner(c, f, bv, plain) + outer(c, f, bv, plain)
            av[c, f] = image
            m0 = m0 + bv[c, f] * bv[c, f]
            m1 = m1 + bv[c, f] * image
            m2 = m2 + image * image
        wait_early[c] = send_time(1, c, av, True)
        if c == 0:
            wait_late[c] = send_time(1, c, av, False)
        wait_side[c] = send_side(1, c, av)
        if c == chans - 1:
            for other in range(1, chans):
                wait_late[other] = send_time(1, other, av, False)
        m0, m1, m2 = whole_sum(m0), whole_sum(m1), whole_sum(m2)
        share = jnp.where(m2 > 0.0, m1 / jnp.where(m2 > 0.0, m2, 1.0), 0.0)
        e0, e1 = 0.0, 0.0
        for f in range(frames):
            rest = bv[c, f] - share * av[c, f]
            e0 = e0 + rest * rest
            e1 = e1 + rest * av[c, f]
        for q, value in enumerate((m0, m1, m2, share, whole_sum(e0), whole_sum(e1))):
            values[q, c] = value
    exchange(0, values)

    every = collect(0)
    totals = jnp.sum(every, axis=0, keepdims=True)

    def taken(value, q):
        return pltpu.roll(value, LANES - 8 * q, 1)

    steps = totals / taken(totals, 1)
    gap = steps - taken(every, 3)
    norms = jnp.sum(taken(every, 4) + gap * (gap * taken(every, 2) - 2.0 * taken(every, 5)), axis=0, keepdims=True)
    ratios = norms / totals
    alpha0 = [steps[:, c:c + 1] for c in range(chans)]
    norm1 = [norms[:, c:c + 1] for c in range(chans)]
    beta = [ratios[:, c:c + 1] for c in range(chans)]

    def combined(ref, side, c, *index):
        own = ref[(0, side, c) + index]
        return (own - alpha0[c] * ref[(1, side, c) + index]) + beta[c] * own

    products = []
    for c in range(chans):
        for f in range(frames):
            residual = bv[c, f] - alpha0[c] * av[c, f]
            rv[c, f] = residual
            pv[c, f] = residual + beta[c] * bv[c, f]
        for copy in wait_side[c]:
            copy.wait_recv()
        product = 0.0
        for f in range(frames):
            image = inner(c, f, pv, lambda ref, *index: combined(ref, *index))
            qv[c, f] = image
            product = product + pv[c, f] * image
        products.append(product[:half] + product[half:])
    for c in range(chans):
        for copy in wait_early[c]:
            copy.wait_recv()
        upper, lower = slice(0, half), slice(half, rows)
        prior = pv[c, 0, upper] - combined(hz, 0, c, upper)
        after = pv[c, frames - 1, lower] - combined(hz, 1, c, lower)
        products[c] = products[c] + hwt[upper] * prior * prior + wtv[frames - 1, lower] * after * after
    exchange(1, {(0, c): whole_sum(products[c]) for c in range(chans)})
    for c in range(chans):
        for copy in wait_late[c]:
            copy.wait_recv()
        for f in sorted({0, frames - 1}):
            qv[c, f] = qv[c, f] + outer(c, f, pv, combined)
    curvatures = jnp.sum(collect(1), axis=0, keepdims=True)
    for c in range(chans):
        alpha1 = norm1[c] / curvatures[:, c:c + 1]
        for f in range(frames):
            x_out[c, f] = alpha0[c] * bv[c, f] + alpha1 * pv[c, f]
            r_out[c, f] = rv[c, f] - alpha1 * qv[c, f]
    for copy in sends:
        copy.wait_send()


def shards(sizes, right_side, screening, time_weight, row_weight, column_weight):
    tms, bands, strips = sizes
    chans, frames, rows, cols = right_side.shape
    f32 = jnp.float32
    field = pltpu.VMEM((chans, frames, rows, cols), f32)
    coefficient = pltpu.VMEM((frames, rows, cols), f32)
    tall = -(-2 * frames // 8) * 8
    devices = tms * bands * strips
    dma = pltpu.SemaphoreType.DMA
    anywhere = pl.BlockSpec(memory_space=pltpu.HBM)
    inside = pl.BlockSpec(memory_space=pltpu.VMEM)
    shape = jax.ShapeDtypeStruct(right_side.shape, f32)
    return pl.pallas_call(
        functools.partial(kernel, sizes),
        out_shape=(shape, shape),
        in_specs=[anywhere] * 5,
        out_specs=(inside, inside),
        scratch_shapes=[field] + [coefficient] * 6 + [field] * 4 + [
            pltpu.VMEM((2, 2, chans, rows, cols), f32),
            pltpu.VMEM((rows, cols), f32),
            pltpu.VMEM((2, 2, chans, tall, cols), f32),
            pltpu.VMEM((2, 2, chans, tall, cols), f32),
            pltpu.VMEM((2, 2, chans, frames, rows, LANES), f32),
            pltpu.VMEM((frames, rows, LANES), f32),
            pltpu.VMEM((2, devices, 1, LANES), f32),
            dma((5,)),
            dma((2, 2, chans, 2)), dma((2, 2, chans, 2)), dma, dma,
            dma((2, 2, chans)), dma((2, 2, chans)),
            dma((2, 2, chans)), dma((2, 2, chans)), dma, dma,
            dma((2, devices)), dma((2, devices)),
        ],
        compiler_params=pltpu.CompilerParams(
            collective_id=0, has_side_effects=True, vmem_limit_bytes=VMEM_BYTES),
        cost_estimate=pl.CostEstimate(flops=10_000_000, bytes_accessed=2_000_000, transcendentals=0),
    )(right_side, screening, time_weight, row_weight, column_weight)


def solution(mesh):
    field = P(None, ("clip", "tm"), "row", "col")
    coefficient = P(("clip", "tm"), "row", "col")
    sizes = tuple(mesh.shape[a] for a in ("tm", "row", "col"))
    return jax.shard_map(
        functools.partial(shards, sizes),
        mesh=mesh,
        in_specs=(field,) + (coefficient,) * 4,
        out_specs=(field, field),
        check_vma=False,
    )
```

time: 49.8 us -> 38.9 us (0.78)
  Pallas kernels: 42.8 us -> 35.5 us
  local copies, waits for them, and re-layouts: 6.1 us -> 2.58 us
    pallas_call x1, Pallas kernels: 42.8 us -> 35.5 us  [shards(): pl.pallas_call(functools.partial(kernel, sizes), out_shape=(shape, shape)...]
    unnamed x12 -> x4, local copies, waits for them, and re-layouts: 6.1 us -> 2.58 us
where the time goes in v2:
time: 38.9 us; the launch traced here: 38.7 us
  Pallas kernels  35.5 us (91%)
  local copies, waits for them, and re-layouts  2.58 us (7%)
  between operations  0.65 us (2%)
    pallas_call x1, Pallas kernels, shards(): pl.pallas_call(functools.partial(kernel, sizes), out_shape=(shape, shape)...  35.5 us
    unnamed x4, local copies, waits for them, and re-layouts  2.58 us

profile of v2, /device:TPU:0, one launch (start us, length us, event | category | flops | bytes accessed | tf_op | source)
XLA Modules:
  0.0 38.7 jit_solution(1425302129902888155)
XLA Ops:
  0.6 35.5 %shard_map.68 = (f32[3,2,32,512]{3,2,1,0:T(8,128)}, f32[3,2,32,512]{3,2,1,0:T(8,128)}) custom-call(f32[3,2,32,512]{3,2,1,0:T(8,128)} %b.1, f32[2,32,512]{2,1,0:T(8,128)} %s.1, f32[2,32,512]{2,1,0:T(8,128)} %wt.1, f32[2,32,512]{2,1,0:T(8,128)} %wy.1, f32[2,32,512]{2,1,0:T(8,128)} %wx.1), custom_call_target="tpu_custom_call" | custom-call | flops 10000000 | bytes 2000000 | tf_op jit(solution)/shard_map/pallas_call | solution.py:266
  36.1 0.0 copy-start
  36.1 1.8 %copy.9 = f32[3,2,32,512]{3,2,1,0:T(8,128)} copy(f32[3,2,32,512]{3,2,1,0:T(8,128)} %get-tuple-element.4) | data formatting | bytes 786432
  38.0 0.0 copy-done
  38.0 0.7 %copy.10 = f32[3,2,32,512]{3,2,1,0:T(8,128)} copy(f32[3,2,32,512]{3,2,1,0:T(8,128)S(1)} %copy-done) | data formatting | bytes 786432
Async XLA Ops:
  36.1 1.8 %copy-start = (f32[3,2,32,512]{3,2,1,0:T(8,128)S(1)}, f32[3,2,32,512]{3,2,1,0:T(8,128)}, u32[]{:S(2)}) copy-start(f32[3,2,32,512]{3,2,1,0:T(8,128)} %get-tuple-element.5) | copy-start | bytes 1179652

commit v3 on v2

--- a/solution.py
+++ b/solution.py
@@ -251,6 +251,14 @@
         copy.wait_send()
 
 
+def written(x, r, x_out, r_out, sem):
+    copies = [pltpu.make_async_copy(v, h, sem.at[i]) for i, (v, h) in enumerate(((x, x_out), (r, r_out)))]
+    for copy in copies:
+        copy.start()
+    for copy in copies:
+        copy.wait()
+
+
 def shards(sizes, right_side, screening, time_weight, row_weight, column_weight):
     tms, bands, strips = sizes
     chans, frames, rows, cols = right_side.shape
@@ -263,9 +271,9 @@
     anywhere = pl.BlockSpec(memory_space=pltpu.HBM)
     inside = pl.BlockSpec(memory_space=pltpu.VMEM)
     shape = jax.ShapeDtypeStruct(right_side.shape, f32)
-    return pl.pallas_call(
+    results = pl.pallas_call(
         functools.partial(kernel, sizes),
-        out_shape=(shape, shape),
+        out_shape=(pltpu.VMEM(right_side.shape, f32),) * 2,
         in_specs=[anywhere] * 5,
         out_specs=(inside, inside),
         scratch_shapes=[field] + [coefficient] * 6 + [field] * 4 + [
@@ -286,6 +294,13 @@
             collective_id=0, has_side_effects=True, vmem_limit_bytes=VMEM_BYTES),
         cost_estimate=pl.CostEstimate(flops=10_000_000, bytes_accessed=2_000_000, transcendentals=0),
     )(right_side, screening, time_weight, row_weight, column_weight)
+    return pl.pallas_call(
+        written,
+        out_shape=(shape, shape),
+        in_specs=[inside] * 2,
+        out_specs=(anywhere, anywhere),
+        scratch_shapes=[dma((2,))],
+    )(*results)
 
 
 def solution(mesh):

time: 38.9 us -> 38.9 us (level)
  Pallas kernels: 35.5 us -> 36.6 us
  local copies, waits for them, and re-layouts: 2.58 us -> 1.5 us
    pallas_call x1 -> x2, Pallas kernels: 35.5 us -> 36.6 us  [the longest x1 34.6 us: shards(): pl.pallas_call(functools.partial(kernel, sizes), out_shape=(pltpu.VMEM(ri...]
    unnamed x4, local copies, waits for them, and re-layouts: 2.58 us -> 1.5 us
where the time goes in v3:
time: 38.9 us; the launch traced here: 38.8 us
  Pallas kernels  36.6 us (94%)
  local copies, waits for them, and re-layouts  1.5 us (4%)
  between operations  0.65 us (2%)
    pallas_call x1, Pallas kernels, shards(): pl.pallas_call(functools.partial(kernel, sizes), out_shape=(pltpu.VMEM(ri...  34.6 us
    pallas_call x1, Pallas kernels, shards(): pl.pallas_call(written, out_shape=(shape, shape), in_specs=[inside] * 2,...  2 us
    unnamed x4, local copies, waits for them, and re-layouts  1.5 us

profile of v3, /device:TPU:0, one launch (start us, length us, event | category | flops | bytes accessed | tf_op | source)
XLA Modules:
  0.0 38.8 jit_solution(257093455422558322)
XLA Ops:
  0.6 34.6 %shard_map.68 = (f32[3,2,32,512]{3,2,1,0:T(8,128)S(1)}, f32[3,2,32,512]{3,2,1,0:T(8,128)S(1)}) custom-call(f32[3,2,32,512]{3,2,1,0:T(8,128)} %b.1, f32[2,32,512]{2,1,0:T(8,128)} %s.1, f32[2,32,512]{2,1,0:T(8,128)} %wt.1, f32[2,32,512]{2,1,0:T(8,128)} %wy.1, f32[2,32,512]{2,1,0:T(8,128)} %wx.1), custom_call_target="tpu_custom_call" | custom-call | flops 10000000 | bytes 2000000 | tf_op jit(solution)/shard_map/pallas_call | solution.py:274
  35.2 0.0 copy-start
  35.3 0.7 %copy-done = f32[3,2,32,512]{3,2,1,0:T(8,128)} copy-done((f32[3,2,32,512]{3,2,1,0:T(8,128)}, f32[3,2,32,512]{3,2,1,0:T(8,128)S(1)}, u32[]{:S(2)}) %copy-start) | copy-done | bytes 393240
  36.0 0.0 copy-start.1
  36.0 0.7 %copy-done.1 = f32[3,2,32,512]{3,2,1,0:T(8,128)} copy-done((f32[3,2,32,512]{3,2,1,0:T(8,128)}, f32[3,2,32,512]{3,2,1,0:T(8,128)S(1)}, u32[]{:S(2)}) %copy-start.1) | copy-done | bytes 393240
  36.7 2.0 %shard_map.69 = (f32[3,2,32,512]{3,2,1,0:T(8,128)}, f32[3,2,32,512]{3,2,1,0:T(8,128)}) custom-call(f32[3,2,32,512]{3,2,1,0:T(8,128)} %copy-done, f32[3,2,32,512]{3,2,1,0:T(8,128)} %copy-done.1), custom_call_target="tpu_custom_call" | custom-call | tf_op jit(solution)/shard_map/pallas_call | solution.py:297
Async XLA Ops:
  35.2 0.8 %copy-start = (f32[3,2,32,512]{3,2,1,0:T(8,128)}, f32[3,2,32,512]{3,2,1,0:T(8,128)S(1)}, u32[]{:S(2)}) copy-start(f32[3,2,32,512]{3,2,1,0:T(8,128)S(1)} %get-tuple-element.4.x) | copy-start | bytes 1179652
  36.0 0.7 %copy-start.1 = (f32[3,2,32,512]{3,2,1,0:T(8,128)}, f32[3,2,32,512]{3,2,1,0:T(8,128)S(1)}, u32[]{:S(2)}) copy-start(f32[3,2,32,512]{3,2,1,0:T(8,128)S(1)} %get-tuple-element.5.r) | copy-start | bytes 1179652

commit v4 on v2

--- a/solution.py
+++ b/solution.py
@@ -13,7 +13,7 @@
 
 
 def kernel(sizes, b, s, wt, wy, wx, x_out, r_out,
-           bv, sv, wtv, wyv, wxv, byv, bxv, av, rv, pv, qv,
+           bv, sv, wtv, wyv, wxv, byv, bxv, av, rv, pv, qv, iv,
            hz, hwt, srow, hrow, hcol, hwx, part,
            load_sem, z_send, z_recv, wt_send, wt_recv, row_send, row_recv,
            col_send, col_recv, wx_send, wx_recv, sum_send, sum_recv):
@@ -40,8 +40,8 @@
         copy.start()
 
     group = []
-    for t in range(tms):
-        for i in range(bands):
+    for t in sorted(range(tms), reverse=True):
+        for i in sorted(range(bands), reverse=True):
             for j in range(strips):
                 if t or i or j:
                     where = (lax.rem(me_t + t, tms), lax.rem(me_r + i, bands), lax.rem(me_c + j, strips))
@@ -159,25 +159,28 @@
     def plain(ref, *index):
         return ref[(0,) + index]
 
+    def second(ref, *index):
+        return ref[(1,) + index]
+
     for copy in loads[3:]:
         copy.wait()
-    weight.wait_recv()
     strip.wait_recv()
     wait_side, wait_early, wait_late, values = {}, {}, {}, {}
     for c in range(chans):
-        for copy in wait_b[c]:
+        for copy in wait_b[c][2:]:
             copy.wait_recv()
         if c == 0:
             for f in range(frames):
                 byv[f] = before_row(wyv[f], hrow[0, 0, 0, frames + f:frames + f + 1])
                 bxv[f] = before_col(wxv[f], hwx[f])
-        m0, m1, m2 = 0.0, 0.0, 0.0
-        for f in range(frames):
-            image = inner(c, f, bv, plain) + outer(c, f, bv, plain)
-            av[c, f] = image
-            m0 = m0 + bv[c, f] * bv[c, f]
-            m1 = m1 + bv[c, f] * image
-            m2 = m2 + image * image
+        for f in range(frames):
+            iv[c, f] = inner(c, f, bv, plain)
+    weight.wait_recv()
+    for c in range(chans):
+        for copy in wait_b[c][:2]:
+            copy.wait_recv()
+        for f in range(frames):
+            av[c, f] = iv[c, f] + outer(c, f, bv, plain)
         wait_early[c] = send_time(1, c, av, True)
         if c == 0:
             wait_late[c] = send_time(1, c, av, False)
@@ -185,6 +188,11 @@
         if c == chans - 1:
             for other in range(1, chans):
                 wait_late[other] = send_time(1, other, av, False)
+        m0, m1, m2 = 0.0, 0.0, 0.0
+        for f in range(frames):
+            m0 = m0 + bv[c, f] * bv[c, f]
+            m1 = m1 + bv[c, f] * av[c, f]
+            m2 = m2 + av[c, f] * av[c, f]
         m0, m1, m2 = whole_sum(m0), whole_sum(m1), whole_sum(m2)
         share = jnp.where(m2 > 0.0, m1 / jnp.where(m2 > 0.0, m2, 1.0), 0.0)
         e0, e1 = 0.0, 0.0
@@ -195,6 +203,11 @@
         for q, value in enumerate((m0, m1, m2, share, whole_sum(e0), whole_sum(e1))):
             values[q, c] = value
     exchange(0, values)
+    for c in range(chans):
+        for copy in wait_side[c]:
+            copy.wait_recv()
+        for f in range(frames):
+            qv[c, f] = inner(c, f, av, second)
 
     every = collect(0)
     totals = jnp.sum(every, axis=0, keepdims=True)
@@ -220,11 +233,9 @@
             residual = bv[c, f] - alpha0[c] * av[c, f]
             rv[c, f] = residual
             pv[c, f] = residual + beta[c] * bv[c, f]
-        for copy in wait_side[c]:
-            copy.wait_recv()
         product = 0.0
         for f in range(frames):
-            image = inner(c, f, pv, lambda ref, *index: combined(ref, *index))
+            image = (iv[c, f] - alpha0[c] * qv[c, f]) + beta[c] * iv[c, f]
             qv[c, f] = image
             product = product + pv[c, f] * image
         products.append(product[:half] + product[half:])
@@ -235,19 +246,22 @@
         prior = pv[c, 0, upper] - combined(hz, 0, c, upper)
         after = pv[c, frames - 1, lower] - combined(hz, 1, c, lower)
         products[c] = products[c] + hwt[upper] * prior * prior + wtv[frames - 1, lower] * after * after
+    before = list(sends)
     exchange(1, {(0, c): whole_sum(products[c]) for c in range(chans)})
     for c in range(chans):
         for copy in wait_late[c]:
             copy.wait_recv()
         for f in sorted({0, frames - 1}):
             qv[c, f] = qv[c, f] + outer(c, f, pv, combined)
+    for copy in before:
+        copy.wait_send()
     curvatures = jnp.sum(collect(1), axis=0, keepdims=True)
     for c in range(chans):
         alpha1 = norm1[c] / curvatures[:, c:c + 1]
         for f in range(frames):
             x_out[c, f] = alpha0[c] * bv[c, f] + alpha1 * pv[c, f]
             r_out[c, f] = rv[c, f] - alpha1 * qv[c, f]
-    for copy in sends:
+    for copy in sends[len(before):]:
         copy.wait_send()
 
 
@@ -262,13 +276,12 @@
     dma = pltpu.SemaphoreType.DMA
     anywhere = pl.BlockSpec(memory_space=pltpu.HBM)
     inside = pl.BlockSpec(memory_space=pltpu.VMEM)
-    shape = jax.ShapeDtypeStruct(right_side.shape, f32)
     return pl.pallas_call(
         functools.partial(kernel, sizes),
-        out_shape=(shape, shape),
+        out_shape=(pltpu.VMEM(right_side.shape, f32),) * 2,
         in_specs=[anywhere] * 5,
         out_specs=(inside, inside),
-        scratch_shapes=[field] + [coefficient] * 6 + [field] * 4 + [
+        scratch_shapes=[field] + [coefficient] * 6 + [field] * 5 + [
             pltpu.VMEM((2, 2, chans, rows, cols), f32),
             pltpu.VMEM((rows, cols), f32),
             pltpu.VMEM((2, 2, chans, tall, cols), f32),

time: 38.9 us -> 36.4 us (0.936)
  Pallas kernels: 35.5 us -> 34.1 us
  local copies, waits for them, and re-layouts: 2.58 us -> 1.49 us
    pallas_call x1, Pallas kernels: 35.5 us -> 34.1 us  [shards(): pl.pallas_call(functools.partial(kernel, sizes), out_shape=(pltpu.VMEM(ri...]
    unnamed x4 -> x2, local copies, waits for them, and re-layouts: 2.58 us -> 1.49 us
where the time goes in v4:
time: 36.4 us; the launch traced here: 36.3 us
  Pallas kernels  34.1 us (94%)
  local copies, waits for them, and re-layouts  1.49 us (4%)
  between operations  0.64 us (2%)
    pallas_call x1, Pallas kernels, shards(): pl.pallas_call(functools.partial(kernel, sizes), out_shape=(pltpu.VMEM(ri...  34.1 us
    unnamed x2, local copies, waits for them, and re-layouts  1.49 us

profile of v4, /device:TPU:0, one launch (start us, length us, event | category | flops | bytes accessed | tf_op | source)
XLA Modules:
  0.0 36.3 jit_solution(11751231434888298216)
XLA Ops:
  0.6 34.1 %shard_map.68 = (f32[3,2,32,512]{3,2,1,0:T(8,128)S(1)}, f32[3,2,32,512]{3,2,1,0:T(8,128)S(1)}) custom-call(f32[3,2,32,512]{3,2,1,0:T(8,128)} %b.1, f32[2,32,512]{2,1,0:T(8,128)} %s.1, f32[2,32,512]{2,1,0:T(8,128)} %wt.1, f32[2,32,512]{2,1,0:T(8,128)} %wy.1, f32[2,32,512]{2,1,0:T(8,128)} %wx.1), custom_call_target="tpu_custom_call" | custom-call | flops 10000000 | bytes 2000000 | tf_op jit(solution)/shard_map/pallas_call | solution.py:279
  34.8 0.7 %copy.9 = f32[3,2,32,512]{3,2,1,0:T(8,128)} copy(f32[3,2,32,512]{3,2,1,0:T(8,128)S(1)} %get-tuple-element.2) | data formatting | bytes 786432
  35.5 0.7 %copy.10 = f32[3,2,32,512]{3,2,1,0:T(8,128)} copy(f32[3,2,32,512]{3,2,1,0:T(8,128)S(1)} %get-tuple-element.3) | data formatting | bytes 786432

commit v5 on v4

--- a/solution.py
+++ b/solution.py
@@ -182,12 +182,7 @@
         for f in range(frames):
             av[c, f] = iv[c, f] + outer(c, f, bv, plain)
         wait_early[c] = send_time(1, c, av, True)
-        if c == 0:
-            wait_late[c] = send_time(1, c, av, False)
         wait_side[c] = send_side(1, c, av)
-        if c == chans - 1:
-            for other in range(1, chans):
-                wait_late[other] = send_time(1, other, av, False)
         m0, m1, m2 = 0.0, 0.0, 0.0
         for f in range(frames):
             m0 = m0 + bv[c, f] * bv[c, f]
@@ -209,6 +204,8 @@
         for f in range(frames):
             qv[c, f] = inner(c, f, av, second)
 
+    for c in range(chans):
+        wait_late[c] = send_time(1, c, av, False)
     every = collect(0)
     totals = jnp.sum(every, axis=0, keepdims=True)
 

time: 36.4 us -> 32.7 us (0.90)
  Pallas kernels: 34.1 us -> 30.4 us
    pallas_call x1, Pallas kernels: 34.1 us -> 30.4 us  [shards(): pl.pallas_call(functools.partial(kernel, sizes), out_shape=(pltpu.VMEM(ri...]
where the time goes in v5:
time: 32.7 us; the launch traced here: 32.5 us
  Pallas kernels  30.4 us (93%)
  local copies, waits for them, and re-layouts  1.49 us (5%)
  between operations  0.64 us (2%)
    pallas_call x1, Pallas kernels, shards(): pl.pallas_call(functools.partial(kernel, sizes), out_shape=(pltpu.VMEM(ri...  30.4 us
    unnamed x2, local copies, waits for them, and re-layouts  1.49 us

profile of v5, /device:TPU:0, one launch (start us, length us, event | category | flops | bytes accessed | tf_op | source)
XLA Modules:
  0.0 32.5 jit_solution(16438172413638526693)
XLA Ops:
  0.6 30.4 %shard_map.68 = (f32[3,2,32,512]{3,2,1,0:T(8,128)S(1)}, f32[3,2,32,512]{3,2,1,0:T(8,128)S(1)}) custom-call(f32[3,2,32,512]{3,2,1,0:T(8,128)} %b.1, f32[2,32,512]{2,1,0:T(8,128)} %s.1, f32[2,32,512]{2,1,0:T(8,128)} %wt.1, f32[2,32,512]{2,1,0:T(8,128)} %wy.1, f32[2,32,512]{2,1,0:T(8,128)} %wx.1), custom_call_target="tpu_custom_call" | custom-call | flops 10000000 | bytes 2000000 | tf_op jit(solution)/shard_map/pallas_call | solution.py:276
  31.0 0.7 %copy.9 = f32[3,2,32,512]{3,2,1,0:T(8,128)} copy(f32[3,2,32,512]{3,2,1,0:T(8,128)S(1)} %get-tuple-element.2) | data formatting | bytes 786432
  31.8 0.7 %copy.10 = f32[3,2,32,512]{3,2,1,0:T(8,128)} copy(f32[3,2,32,512]{3,2,1,0:T(8,128)S(1)} %get-tuple-element.3) | data formatting | bytes 786432
